TPU v7x, 32 devices: a whole 2x2x4 slice. The times are simulated.
32 devices in a mesh: groups: 2 (over y), mp: 4 (over x, core), hidden: 4 (over z).
Axes of the slice: x: 2, y: 2, z: 4, core: 2. Of those that a mesh axis runs over, the one named last changes fastest.
Arguments:
- tokens: bfloat16 [768, 8192], P(('groups', 'hidden'), 'mp'), parts along dimension 0, may hold values from -6 to 6
- block_mask: int32 [768, 64], P(('groups', 'hidden'), 'mp'), parts along dimension 0, may hold values from 0 to 1, as said below
- gate_weight: bfloat16 [8192, 26624], P('mp', 'hidden'), may hold values from -0.0625 to 0.0625
- up_weight: bfloat16 [8192, 26624], P('mp', 'hidden'), may hold values from -0.0625 to 0.0625
- down_weight: bfloat16 [26624, 8192], P('hidden', 'mp'), may hold values from -0.0390625 to 0.0390625
Outputs:
- mixed: bfloat16 [768, 8192], P(('groups', 'hidden'), 'mp'), parts along dimension 0
There are 2 independent parts, one for each index of `groups`. A program takes and returns all parts, laid end to end along the dimension named above; an argument that names none is the same for every part. Nothing has to cross between parts.
Inputs may be any that keep to these rules, and one draw needn't show every extreme that they name: `block_mask`: each row has exactly 25 active blocks; some blocks are active in far more rows than others.
All inputs are finite; a program needn't handle non-finite values.
Results may differ from a plain program's by a relative error of at most 0.0051.
Values may be sent and summed in bfloat16 or wider, within the bound.
A program may use at most 256 MiB of HBM per device.

v0:
```python
import jax
import jax.numpy as jnp
from jax import lax
from jax.sharding import PartitionSpec as P

BLOCK = 128


def project(pieces, gate_weight, up_weight):
    gate_sum = jnp.dot(pieces, gate_weight, preferred_element_type=jnp.float32)
    up_sum = jnp.dot(pieces, up_weight, preferred_element_type=jnp.float32)
    return (gate_sum, up_sum)


def activate(gate_sum, up_sum):
    return (jax.nn.silu(gate_sum) * up_sum).astype(jnp.bfloat16)


def local(tokens, block_mask, gate_weight, up_weight, down_weight):
    keep = jnp.repeat(block_mask, BLOCK, axis=1).astype(tokens.dtype)
    masked = tokens * keep
    all_rows = lax.all_gather(masked, "hidden", axis=0, tiled=True)
    units = gate_weight.shape[1]
    pieces = all_rows
    gate_sum, up_sum = project(pieces, gate_weight, up_weight)
    summed = lax.psum_scatter(
        jnp.concatenate([gate_sum, up_sum], axis=1), "mp", scatter_dimension=0, tiled=True
    )
    hidden_share = activate(summed[:, :units], summed[:, units:])
    hidden_all = lax.all_gather(hidden_share, "mp", axis=0, tiled=True)
    pieces = hidden_all
    mixed = lax.psum_scatter(
        jnp.dot(pieces, down_weight, preferred_element_type=jnp.float32),
        "hidden",
        scatter_dimension=0,
        tiled=True,
    )
    return mixed.astype(jnp.bfloat16)


def solution(mesh):
    in_specs = (
        P(("groups", "hidden"), "mp"),
        P(("groups", "hidden"), "mp"),
        P("mp", "hidden"),
        P("mp", "hidden"),
        P("hidden", "mp"),
    )
    out_specs = P(("groups", "hidden"), "mp")
    return jax.shard_map(local, mesh=mesh, in_specs=in_specs, out_specs=out_specs, check_vma=False)
```

profile of v0, /device:TPU:8, one launch (start us, length us, event | category | flops | bytes accessed | tf_op | source)
XLA Modules:
  0.0 375.5 jit_solution(10145258229673898300)
XLA Ops:
  6.5 0.0 all-gather.3.cloned.1.call-start
  6.5 0.7 convert_element_type.13
  7.2 0.1 copy.6
  7.4 0.3 broadcast_in_dim.3
  7.6 1.8 bitcast_multiply_fusion
  9.5 0.0 all-gather.3.cloned.1.call-update
  9.5 0.0 reduce-scatter.3.cloned.1.call-start
  9.5 37.3 %all-gather.3.cloned.1.call-done = bf16[384,2048]{1,0:T(8,128)(2,1)} async-done(((bf16[96,2048]{1,0:T(8,128)(2,1)}), bf16[384,2048]{1,0:T(8,128)(2,1)}) %all-gather.3.cloned.1.call-update) | async-done | bytes 1572880 | tf_op jit(solution)/shard_map/all_gather | solution.py:22
  46.9 0.0 copy-start
  46.9 18.6 %fusion.2 = f32[384,6656]{1,0:T(8,128)S(1)} fusion(bf16[384,2048]{1,0:T(8,128)(2,1)} %all-gather.3.cloned.1.call-done, bf16[2048,6656]{1,0:T(8,128)(2,1)} %param.8), kind=kOutput, calls=%fused_computation.5 | convolution fusion | flops 10468982784 | bytes 39059456 | tf_op jit(solution)/shard_map/dot_general | solution.py:11
  65.5 0.0 copy-done
  65.5 18.1 %fusion.1 = f32[384,6656]{1,0:T(8,128)} fusion(bf16[384,2048]{1,0:T(8,128)(2,1)S(1)} %copy-done, bf16[2048,6656]{1,0:T(8,128)(2,1)} %param.7), kind=kOutput, calls=%fused_computation.4 | convolution fusion | flops 10468982784 | bytes 39059456 | tf_op jit(solution)/shard_map/dot_general | solution.py:10
  83.6 11.2 %pad_maximum_fusion = f32[384,13312]{1,0:T(8,128)} fusion(f32[384,6656]{1,0:T(8,128)S(1)} %fusion.2, f32[384,6656]{1,0:T(8,128)} %fusion.1), kind=kLoop, calls=%fused_computation | loop fusion | flops 5111808 | bytes 40894464 | tf_op jit(solution)/shard_map/concatenate | solution.py:27
  94.8 0.0 reduce-scatter.3.cloned.1.call-update
  94.8 0.0 all-gather.5.cloned.1.call-start
  94.9 149.7 %reduce-scatter.3.cloned.1.call-done = f32[96,13312]{1,0:T(8,128)} async-done(((f32[384,13312]{1,0:T(8,128)}), f32[96,13312]{1,0:T(8,128)}) %reduce-scatter.3.cloned.1.call-update) | async-done | bytes 5111824 | tf_op jit(solution)/shard_map/reduce_scatter | solution.py:26
  244.6 4.2 %fusion = bf16[96,6656]{1,0:T(8,128)(2,1)} fusion(f32[96,13312]{1,0:T(8,128)} %reduce-scatter.3.cloned.1.call-done), kind=kLoop, calls=%fused_computation.2 | loop fusion | flops 3833856 | bytes 6389760 | tf_op jit(solution)/shard_map/convert_element_type | solution.py:16
  248.8 0.0 all-gather.5.cloned.1.call-update
  248.8 0.2 reduce-scatter.5.cloned.1.call-start
  249.1 39.6 %all-gather.5.cloned.1.call-done = bf16[384,6656]{1,0:T(8,128)(2,1)} async-done(((bf16[96,6656]{1,0:T(8,128)(2,1)}), bf16[384,6656]{1,0:T(8,128)(2,1)}) %all-gather.5.cloned.1.call-update) | async-done | bytes 5111824 | tf_op jit(solution)/shard_map/all_gather | solution.py:30
  288.7 18.4 %fusion.3 = f32[384,2048]{1,0:T(8,128)} fusion(bf16[384,6656]{1,0:T(8,128)(2,1)} %all-gather.5.cloned.1.call-done, bf16[6656,2048]{1,0:T(8,128)(2,1)} %param.9), kind=kOutput, calls=%fused_computation.6 | convolution fusion | flops 10468982784 | bytes 35520512 | tf_op jit(solution)/shard_map/dot_general | solution.py:33
  307.1 0.0 reduce-scatter.5.cloned.1.call-update
  307.1 59.9 %reduce-scatter.5.cloned.1.call-done = f32[96,2048]{1,0:T(8,128)} async-done(((f32[384,2048]{1,0:T(8,128)}), f32[96,2048]{1,0:T(8,128)}) %reduce-scatter.5.cloned.1.call-update) | async-done | bytes 786448 | tf_op jit(solution)/shard_map/reduce_scatter | solution.py:32
  367.1 1.9 convert_element_type.16
Async XLA Ops:
  6.5 40.3 %all-gather.3.cloned.1.call-start = ((), (), s32[]{:S(2)}) async-start(), calls=%async_computation.2 | async-start | bytes 1966080 | tf_op jit(solution)/shard_map/all_gather | solution.py:22
  9.5 235.1 %reduce-scatter.3.cloned.1.call-start = ((), (), s32[]{:S(2)}) async-start(), calls=%async_computation.3 | async-start | bytes 25559040 | tf_op jit(solution)/shard_map/reduce_scatter | solution.py:26
  46.9 18.6 %copy-start = (bf16[384,2048]{1,0:T(8,128)(2,1)S(1)}, bf16[384,2048]{1,0:T(8,128)(2,1)}, u32[]{:S(2)}) copy-start(bf16[384,2048]{1,0:T(8,128)(2,1)} %all-gather.3.cloned.1.call-done) | copy-start | bytes 4718596
  94.8 193.8 %all-gather.5.cloned.1.call-start = ((), (), s32[]{:S(2)}) async-start(), calls=%async_computation.4 | async-start | bytes 6389760 | tf_op jit(solution)/shard_map/all_gather | solution.py:30
  248.8 118.2 %reduce-scatter.5.cloned.1.call-start = ((), (), s32[]{:S(2)}) async-start(), calls=%async_computation.5 | async-start | bytes 3932160 | tf_op jit(solution)/shard_map/reduce_scatter | solution.py:32
Sparse Core Ops, SparseCore 0:
  9.6 37.2 all-gather.2
  95.0 149.5 reduce-scatter.2
  249.0 39.6 all-gather.4
  307.2 59.7 reduce-scatter.4
where the time goes:
time: 378 us; the launch traced here: 376 us
  waiting for transfers between devices  287 us (76%)
  matrix products  55.1 us (15%)
  other arithmetic  19.9 us (5%)
  between operations  13.2 us (3%)
    reduce_scatter x1, waiting for transfers between devices, local(): lax.psum_scatter(jnp.concatenate([gate_sum, up_sum], axis=1), 'mp', scatt...  150 us
    reduce_scatter x1, waiting for transfers between devices, local(): lax.psum_scatter(jnp.dot(pieces, down_weight, preferred_element_type=jnp....  59.9 us
    all_gather x1, waiting for transfers between devices, local(): hidden_all = lax.all_gather(hidden_share, 'mp', axis=0, tiled=True)  39.6 us
    all_gather x1, waiting for transfers between devices, local(): all_rows = lax.all_gather(masked, 'hidden', axis=0, tiled=True)  37.3 us
    dot_general x1, matrix products, project(): up_sum = jnp.dot(pieces, up_weight, preferred_element_type=jnp.float32)  18.6 us
    dot_general x1, matrix products, local(): jnp.dot(pieces, down_weight, preferred_element_type=jnp.float32)  18.4 us
    dot_general x1, matrix products, project(): gate_sum = jnp.dot(pieces, gate_weight, preferred_element_type=jnp.float32)  18.1 us
    concatenate x1, other arithmetic, local(): jnp.concatenate([gate_sum, up_sum], axis=1)  11.2 us
  transfers between devices with their start and end apart: 4, of which 4 were waited for; matrix products, arithmetic and copies ran while one was open for 0% of the time, Pallas kernels for 0%

commit v1 on v0

v1 whole, which is shorter than its diff:
```python
import jax
import jax.numpy as jnp
import numpy as np
from jax import lax
from jax.sharding import PartitionSpec as P

BLOCK = 128
CHUNKS = 5


def widths(units):
    step = 256
    tiles = units // step
    parts = min(CHUNKS, tiles)
    sizes = [(tiles // parts + (1 if i < tiles % parts else 0)) * step for i in range(parts)]
    sizes[-1] += units - sum(sizes)
    return sizes


def local(tokens, block_mask, gate_weight, up_weight, down_weight):
    n = lax.axis_size("mp")
    z = lax.axis_size("hidden")
    me = lax.axis_index("mp")
    mz = lax.axis_index("hidden")
    rows, features = tokens.shape
    cols = down_weight.shape[1]
    units = gate_weight.shape[1]
    r = rows // n
    bits = [1 << i for i in range(n.bit_length() - 1)]
    masks = np.array(
        [sum(b for l, b in enumerate(bits) if not (p >> (len(bits) - 1 - l)) & 1) for p in range(n)], np.int32
    )
    inverse = np.argsort(masks).astype(np.int32)

    def swap(x, bit):
        return lax.ppermute(x, "mp", [(i, i ^ bit) for i in range(n)])

    keep = jnp.repeat(block_mask, BLOCK, axis=1).astype(tokens.dtype)
    masked = (tokens * keep).reshape(n, r, features)
    masked = jnp.take(masked, me ^ jnp.asarray(masks), axis=0)
    all_rows = lax.all_gather(masked, "hidden", axis=1, tiled=True).reshape(n * z * r, features)

    acc = None
    start = 0
    for width in widths(units):
        stop = start + width
        gate = jnp.dot(all_rows, gate_weight[:, start:stop], preferred_element_type=jnp.float32)
        up = jnp.dot(all_rows, up_weight[:, start:stop], preferred_element_type=jnp.float32)
        for bit in bits:
            half = gate.shape[0] // 2
            sent = jnp.concatenate([gate[:half].astype(jnp.bfloat16), up[:half].astype(jnp.bfloat16)], axis=0)
            got = swap(sent, bit)
            gate = gate[half:] + got[:half].astype(jnp.float32)
            up = up[half:] + got[half:].astype(jnp.float32)
        hidden = (jax.nn.silu(gate) * up).astype(jnp.bfloat16)
        for bit in reversed(bits):
            hidden = jnp.concatenate([swap(hidden, bit), hidden], axis=0)
        part = jnp.dot(hidden, down_weight[start:stop], preferred_element_type=jnp.float32)
        acc = part if acc is None else acc + part
        start = stop

    acc = acc.reshape(n, z, r, cols)
    total = lax.dynamic_index_in_dim(acc, mz, 1, keepdims=False)
    for s in range(1, z):
        block = lax.dynamic_index_in_dim(acc, (mz + s) % z, 1, keepdims=False).astype(jnp.bfloat16)
        got = lax.ppermute(block, "hidden", [(i, (i + s) % z) for i in range(z)])
        total = total + got.astype(jnp.float32)
    total = jnp.take(total.astype(jnp.bfloat16), jnp.asarray(inverse)[me ^ jnp.arange(n)], axis=0)
    return total.reshape(rows, cols)


def solution(mesh):
    in_specs = (
        P(("groups", "hidden"), "mp"),
        P(("groups", "hidden"), "mp"),
        P("mp", "hidden"),
        P("mp", "hidden"),
        P("hidden", "mp"),
    )
    out_specs = P(("groups", "hidden"), "mp")
    return jax.shard_map(local, mesh=mesh, in_specs=in_specs, out_specs=out_specs, check_vma=False)
```

time: 378 us -> 258 us (0.68)
  waiting for transfers between devices: 287 us -> 140 us
  starting transfers between devices: 0.31 us -> 19.2 us
  matrix products: 55.1 us -> 71.6 us
  other arithmetic: 19.9 us -> 8.34 us
    reduce_scatter x2 -> x0, waiting for transfers between devices: 210 us -> none  [the longest x1 150 us: local(): lax.psum_scatter(jnp.concatenate([gate_sum, up_sum], axis=1), 'mp', scatt...]
    ppermute x0 -> x23, waiting for transfers between devices: none -> 103 us  [the longest x20 69 us: swap(): return lax.ppermute(x, 'mp', [(i, i ^ bit) for i in range(n)])]
    all_gather x2 -> x1, waiting for transfers between devices: 77 us -> 36.7 us  [local(): lax.all_gather(masked, 'hidden', axis=1, tiled=True)]
    ppermute x0 -> x23, starting transfers between devices: none -> 19.2 us  [the longest x20 15.3 us: swap(): return lax.ppermute(x, 'mp', [(i, i ^ bit) for i in range(n)])]
    dot_general x3 -> x15, matrix products: 55.1 us -> 71.6 us  [the longest x5 24.2 us: local(): jnp.dot(all_rows, up_weight[:, start:stop], preferred_element_type=jnp.fl...]
    concatenate x1 -> x15, other arithmetic: 11.2 us -> 0.7 us  [the longest x10 0.53 us: local(): jnp.concatenate([gate[:half].astype(jnp.bfloat16), up[:half].astype(jnp.b...]
  transfers between devices with their start and end apart: 4 -> 24, of which waited for: 4 -> 13; matrix products, arithmetic and copies ran while one was open for 0% -> 11% of each run, Pallas kernels for 0% -> 0%
where the time goes in v1:
time: 258 us; the launch traced here: 257 us
  waiting for transfers between devices  140 us (54%)
  matrix products  71.6 us (28%)
  starting transfers between devices  19.2 us (7%)
  between operations  14 us (5%)
  other arithmetic  8.34 us (3%)
  local copies, waits for them, and re-layouts  4.05 us (2%)
    ppermute x20, waiting for transfers between devices, swap(): return lax.ppermute(x, 'mp', [(i, i ^ bit) for i in range(n)])  69 us
    all_gather x1, waiting for transfers between devices, local(): lax.all_gather(masked, 'hidden', axis=1, tiled=True)  36.7 us
    ppermute x3, waiting for transfers between devices, local(): got = lax.ppermute(block, 'hidden', [(i, (i + s) % z) for i in range(z)])  34.4 us
    dot_general x5, matrix products, local(): jnp.dot(all_rows, up_weight[:, start:stop], preferred_element_type=jnp.fl...  24.2 us
    dot_general x5, matrix products, local(): jnp.dot(hidden, down_weight[start:stop], preferred_element_type=jnp.float32)  23.8 us
    dot_general x5, matrix products, local(): jnp.dot(all_rows, gate_weight[:, start:stop], preferred_element_type=jnp....  23.6 us
    ppermute x20, starting transfers between devices, swap(): return lax.ppermute(x, 'mp', [(i, i ^ bit) for i in range(n)])  15.3 us
  transfers between devices with their start and end apart: 24, of which 13 were waited for; matrix products, arithmetic and copies ran while one was open for 11% of the time, Pallas kernels for 0%

profile of v1, /device:TPU:8, one launch (start us, length us, event | category | flops | bytes accessed | tf_op | source)
XLA Modules:
  0.0 257.3 jit_solution(18430526855586748150)
XLA Ops:
  6.5 0.7 compare_and_fusion.1
  7.3 0.7 convert_element_type.132
  8.4 1.1 bitcast_multiply_fusion
  10.0 0.8 broadcast_select_fusion.1
  11.0 0.6 gather_fusion
  11.6 36.7 %all-gather.2.cloned.1.call-done = bf16[4,96,2048]{2,1,0:T(8,128)(2,1)} async-done(((bf16[4,24,2048]{2,1,0:T(8,128)(2,1)}), bf16[4,96,2048]{2,1,0:T(8,128)(2,1)}) %all-gather.2.cloned.1.call-update) | async-done | bytes 1572880 | tf_op jit(solution)/shard_map/all_gather | solution.py:41
  48.3 5.3 %fusion.8 = f32[384,1280]{1,0:T(8,128)S(1)} fusion(bf16[384,2048]{1,0:T(8,128)(2,1)} %bitcast.45, bf16[2048,6656]{1,0:T(8,128)(2,1)} %param.12), kind=kOutput, calls=%fused_computation.11 | convolution fusion | flops 2013265920 | bytes 8781824 | tf_op jit(solution)/shard_map/dot_general | solution.py:48
  53.7 4.7 %fusion.26 = f32[384,1280]{1,0:T(8,128)S(1)} fusion(bf16[384,2048]{1,0:T(8,128)(2,1)S(1)} %bitcast.46, bf16[2048,6656]{1,0:T(8,128)(2,1)} %param.12), kind=kOutput, calls=%fused_computation.29 | convolution fusion | flops 2013265920 | bytes 8781824 | tf_op jit(solution)/shard_map/dot_general | solution.py:48
  58.4 4.7 %fusion.10 = f32[384,1280]{1,0:T(8,128)S(1)} fusion(bf16[384,2048]{1,0:T(8,128)(2,1)S(1)} %bitcast.47, bf16[2048,6656]{1,0:T(8,128)(2,1)} %param.11), kind=kOutput, calls=%fused_computation.13 | convolution fusion | flops 2013265920 | bytes 8781824 | tf_op jit(solution)/shard_map/dot_general | solution.py:47
  63.1 4.7 %fusion.28 = f32[384,1280]{1,0:T(8,128)S(1)} fusion(bf16[384,2048]{1,0:T(8,128)(2,1)S(1)} %bitcast.48, bf16[2048,6656]{1,0:T(8,128)(2,1)} %param.11), kind=kOutput, calls=%fused_computation.31 | convolution fusion | flops 2013265920 | bytes 8781824 | tf_op jit(solution)/shard_map/dot_general | solution.py:47
  67.8 4.7 %fusion.2 = f32[384,1536]{1,0:T(8,128)S(1)} fusion(bf16[384,2048]{1,0:T(8,128)(2,1)S(1)} %bitcast.49, bf16[2048,6656]{1,0:T(8,128)(2,1)} %param.12), kind=kOutput, calls=%fused_computation.5 | convolution fusion | flops 2415919104 | bytes 10223616 | tf_op jit(solution)/shard_map/dot_general | solution.py:48
  72.5 4.9 %fusion.4 = f32[384,1536]{1,0:T(8,128)S(1)} fusion(bf16[384,2048]{1,0:T(8,128)(2,1)S(1)} %bitcast.50, bf16[2048,6656]{1,0:T(8,128)(2,1)} %param.11), kind=kOutput, calls=%fused_computation.7 | convolution fusion | flops 2415919104 | bytes 10223616 | tf_op jit(solution)/shard_map/dot_general | solution.py:47
  77.4 4.7 %fusion.20 = f32[384,1280]{1,0:T(8,128)S(1)} fusion(bf16[384,2048]{1,0:T(8,128)(2,1)S(1)} %bitcast.51, bf16[2048,6656]{1,0:T(8,128)(2,1)} %param.12), kind=kOutput, calls=%fused_computation.23 | convolution fusion | flops 2013265920 | bytes 8781824 | tf_op jit(solution)/shard_map/dot_general | solution.py:48
  82.1 4.7 %fusion.22 = f32[384,1280]{1,0:T(8,128)S(1)} fusion(bf16[384,2048]{1,0:T(8,128)(2,1)S(1)} %bitcast.52, bf16[2048,6656]{1,0:T(8,128)(2,1)} %param.11), kind=kOutput, calls=%fused_computation.25 | convolution fusion | flops 2013265920 | bytes 8781824 | tf_op jit(solution)/shard_map/dot_general | solution.py:47
  86.8 4.7 %fusion.14 = f32[384,1280]{1,0:T(8,128)S(1)} fusion(bf16[384,2048]{1,0:T(8,128)(2,1)S(1)} %bitcast.53, bf16[2048,6656]{1,0:T(8,128)(2,1)} %param.12), kind=kOutput, calls=%fused_computation.17 | convolution fusion | flops 2013265920 | bytes 8781824 | tf_op jit(solution)/shard_map/dot_general | solution.py:48
  93.6 4.7 %fusion.16 = f32[384,1280]{1,0:T(8,128)S(1)} fusion(bf16[384,2048]{1,0:T(8,128)(2,1)S(1)} %bitcast.54, bf16[2048,6656]{1,0:T(8,128)(2,1)} %param.11), kind=kOutput, calls=%fused_computation.19 | convolution fusion | flops 2013265920 | bytes 8781824 | tf_op jit(solution)/shard_map/dot_general | solution.py:47
  98.8 1.5 collective-permute-start.17
  100.7 0.6 collective-permute-start.5
  101.6 1.5 collective-permute-start.9
  103.4 0.6 collective-permute-start.13
  104.5 1.6 collective-permute-start.1
  106.0 6.9 %collective-permute-done.17 = bf16[192,1280]{1,0:T(8,128)(2,1)S(1)} collective-permute-done((bf16[192,1280]{1,0:T(8,128)(2,1)S(1)}, bf16[192,1280]{1,0:T(8,128)(2,1)S(1)}, u32[]{:S(2)}, u32[]{:S(2)}) %collective-permute-start.17) | collective-permute-done | bytes 491552 | tf_op jit(solution)/shard_map/ppermute | solution.py:36
  113.1 1.5 collective-permute-start.18
  114.6 8.8 %collective-permute-done.5 = bf16[192,1280]{1,0:T(8,128)(2,1)S(1)} collective-permute-done((bf16[192,1280]{1,0:T(8,128)(2,1)S(1)}, bf16[192,1280]{1,0:T(8,128)(2,1)S(1)}, u32[]{:S(2)}, u32[]{:S(2)}) %collective-permute-start.5) | collective-permute-done | bytes 491552 | tf_op jit(solution)/shard_map/ppermute | solution.py:36
  123.6 1.5 collective-permute-start.6
  125.2 8.8 %collective-permute-done.9 = bf16[192,1280]{1,0:T(8,128)(2,1)S(1)} collective-permute-done((bf16[192,1280]{1,0:T(8,128)(2,1)S(1)}, bf16[192,1280]{1,0:T(8,128)(2,1)S(1)}, u32[]{:S(2)}, u32[]{:S(2)}) %collective-permute-start.9) | collective-permute-done | bytes 491552 | tf_op jit(solution)/shard_map/ppermute | solution.py:36
  134.2 1.5 collective-permute-start.10
  135.7 8.8 %collective-permute-done.13 = bf16[192,1280]{1,0:T(8,128)(2,1)S(1)} collective-permute-done((bf16[192,1280]{1,0:T(8,128)(2,1)S(1)}, bf16[192,1280]{1,0:T(8,128)(2,1)S(1)}, u32[]{:S(2)}, u32[]{:S(2)}) %collective-permute-start.13) | collective-permute-done | bytes 491552 | tf_op jit(solution)/shard_map/ppermute | solution.py:36
  144.7 1.5 collective-permute-start.14
  146.2 16.2 %collective-permute-done.18 = bf16[96,1280]{1,0:T(8,128)(2,1)S(1)} collective-permute-done((bf16[96,1280]{1,0:T(8,128)(2,1)S(1)}, bf16[96,1280]{1,0:T(8,128)(2,1)S(1)}, u32[]{:S(2)}, u32[]{:S(2)}) %collective-permute-start.18) | collective-permute-done | bytes 245792 | tf_op jit(solution)/shard_map/ppermute | solution.py:36
  162.5 5.2 %collective-permute-done.6 = bf16[96,1280]{1,0:T(8,128)(2,1)S(1)} collective-permute-done((bf16[96,1280]{1,0:T(8,128)(2,1)S(1)}, bf16[96,1280]{1,0:T(8,128)(2,1)S(1)}, u32[]{:S(2)}, u32[]{:S(2)}) %collective-permute-start.6) | collective-permute-done | bytes 245792 | tf_op jit(solution)/shard_map/ppermute | solution.py:36
  168.0 1.5 collective-permute-start.2
  169.6 3.4 %collective-permute-done.10 = bf16[96,1280]{1,0:T(8,128)(2,1)S(1)} collective-permute-done((bf16[96,1280]{1,0:T(8,128)(2,1)S(1)}, bf16[96,1280]{1,0:T(8,128)(2,1)S(1)}, u32[]{:S(2)}, u32[]{:S(2)}) %collective-permute-start.10) | collective-permute-done | bytes 245792 | tf_op jit(solution)/shard_map/ppermute | solution.py:36
  173.1 5.2 %collective-permute-done.14 = bf16[96,1280]{1,0:T(8,128)(2,1)S(1)} collective-permute-done((bf16[96,1280]{1,0:T(8,128)(2,1)S(1)}, bf16[96,1280]{1,0:T(8,128)(2,1)S(1)}, u32[]{:S(2)}, u32[]{:S(2)}) %collective-permute-start.14) | collective-permute-done | bytes 245792 | tf_op jit(solution)/shard_map/ppermute | solution.py:36
  178.3 5.8 %collective-permute-done.2 = bf16[96,1536]{1,0:T(8,128)(2,1)S(1)} collective-permute-done((bf16[96,1536]{1,0:T(8,128)(2,1)S(1)}, bf16[96,1536]{1,0:T(8,128)(2,1)S(1)}, u32[]{:S(2)}, u32[]{:S(2)}) %collective-permute-start.2) | collective-permute-done | bytes 294944 | tf_op jit(solution)/shard_map/ppermute | solution.py:36
  184.3 4.7 %fusion.24 = f32[384,2048]{1,0:T(8,128)S(1)} fusion(bf16[6656,2048]{1,0:T(8,128)(2,1)} %param.13, bf16[96,1280]{1,0:T(8,128)(2,1)S(1)} %fusion.71, bf16[96,1280]{1,0:T(8,128)(2,1)S(1)} %collective-permute-done.6, bf16[192,1280]{1,0:T(8,128)(2,1)S(1)} %collective-permute-done.7), kind=kOutput, calls=%fused_computation.27 | convolution fusion | flops 2016215040 | bytes 9371648 | tf_op jit(solution)/shard_map/dot_general | solution.py:58
  189.0 4.7 %fusion.18 = f32[384,2048]{1,0:T(8,128)S(1)} fusion(bf16[6656,2048]{1,0:T(8,128)(2,1)} %param.13, bf16[96,1280]{1,0:T(8,128)(2,1)S(1)} %fusion.69, bf16[96,1280]{1,0:T(8,128)(2,1)S(1)} %collective-permute-done.10, bf16[192,1280]{1,0:T(8,128)(2,1)S(1)} %collective-permute-done.11), kind=kOutput, calls=%fused_computation.21 | convolution fusion | flops 2016215040 | bytes 9371648 | tf_op jit(solution)/shard_map/dot_general | solution.py:58
  193.7 4.7 %fusion.12 = f32[384,2048]{1,0:T(8,128)S(1)} fusion(bf16[6656,2048]{1,0:T(8,128)(2,1)} %param.13, bf16[96,1280]{1,0:T(8,128)(2,1)S(1)} %fusion.67, bf16[96,1280]{1,0:T(8,128)(2,1)S(1)} %collective-permute-done.14, bf16[192,1280]{1,0:T(8,128)(2,1)S(1)} %collective-permute-done.15), kind=kOutput, calls=%fused_computation.15 | convolution fusion | flops 2016215040 | bytes 9371648 | tf_op jit(solution)/shard_map/dot_general | solution.py:58
  198.4 4.7 %fusion = f32[384,2048]{1,0:T(8,128)S(1)} fusion(bf16[6656,2048]{1,0:T(8,128)(2,1)} %param.13, bf16[96,1536]{1,0:T(8,128)(2,1)S(1)} %fusion.63, bf16[96,1536]{1,0:T(8,128)(2,1)S(1)} %collective-permute-done.2, bf16[192,1536]{1,0:T(8,128)(2,1)S(1)} %collective-permute-done.3), kind=kOutput, calls=%fused_computation.3 | convolution fusion | flops 2419458048 | bytes 10616832 | tf_op jit(solution)/shard_map/dot_general | solution.py:58
  203.2 5.0 %add_add_fusion = f32[384,2048]{1,0:T(8,128)S(1)} fusion(f32[384,2048]{1,0:T(8,128)S(1)} %fusion.12, f32[384,2048]{1,0:T(8,128)S(1)} %fusion.18, f32[384,2048]{1,0:T(8,128)S(1)} %fusion, f32[384,2048]{1,0:T(8,128)S(1)} %fusion.24, bf16[6656,2048]{1,0:T(8,128)(2,1)} %param.13, bf16[96,1280]{1,0:T(8,128)(2,1)S(1)} %fusion.65, ...), kind=kOutput, calls=%fused_computation.33 | convolution fusion | flops 2019360768 | bytes 21954560 | tf_op jit(solution)/shard_map/dot_general | solution.py:58
  208.2 1.0 fusion.73
  209.2 1.4 collective-permute-start.20
  210.6 2.5 collective-permute-start.21
  213.2 8.3 %collective-permute-done.20 = bf16[4,24,2048]{2,1,0:T(8,128)(2,1)} collective-permute-done((bf16[4,24,2048]{2,1,0:T(8,128)(2,1)}, bf16[4,24,2048]{2,1,0:T(8,128)(2,1)}, u32[]{:S(2)}, u32[]{:S(2)}) %collective-permute-start.20) | collective-permute-done | bytes 393248 | tf_op jit(solution)/shard_map/ppermute | solution.py:66
  221.5 23.8 %collective-permute-done.21 = bf16[4,24,2048]{2,1,0:T(8,128)(2,1)} collective-permute-done((bf16[4,24,2048]{2,1,0:T(8,128)(2,1)}, bf16[4,24,2048]{2,1,0:T(8,128)(2,1)}, u32[]{:S(2)}, u32[]{:S(2)}) %collective-permute-start.21) | collective-permute-done | bytes 393248 | tf_op jit(solution)/shard_map/ppermute | solution.py:66
  245.2 2.3 collective-permute-done.22
  247.6 1.4 fusion.61
  249.6 0.8 broadcast_select_fusion
  (83 shorter events, 6.8 us)
Async XLA Ops:
  6.5 4.5 %copy-start = (s32[4]{0:T(128)S(1)}, s32[4]{0:T(128)}, u32[]{:S(2)}) copy-start(s32[4]{0:T(128)} %constant.65.clone) | copy-start | bytes 52
  6.5 41.8 %all-gather.2.cloned.1.call-start = ((), (), s32[]{:S(2)}) async-start(), calls=%async_computation | async-start | bytes 1966080 | tf_op jit(solution)/shard_map/all_gather | solution.py:41
  48.3 5.4 %copy-start.1 = (bf16[4,96,2048]{2,1,0:T(8,128)(2,1)S(1)}, bf16[4,96,2048]{2,1,0:T(8,128)(2,1)}, u32[]{:S(2)}) copy-start(bf16[4,96,2048]{2,1,0:T(8,128)(2,1)} %all-gather.2.cloned.1.call-done) | copy-start | bytes 4718596
  91.7 6.8 %collective-permute-start.16 = (bf16[384,1280]{1,0:T(8,128)(2,1)S(1)}, bf16[384,1280]{1,0:T(8,128)(2,1)S(1)}, u32[]{:S(2)}, u32[]{:S(2)}) collective-permute-start(bf16[384,1280]{1,0:T(8,128)(2,1)S(1)} %pad_maximum_fusion.4), channel_id=1, source_target_pairs={{0,4},{4,0},{8,12},{12,8},{1,5},{5,1},{9,13},{13,9},{2,6},{6,2},{1... | collective-permute-start | bytes 2949128 | tf_op jit(solution)/shard_map/ppermute | solution.py:36
  92.0 8.4 %collective-permute-start.4 = (bf16[384,1280]{1,0:T(8,128)(2,1)S(1)}, bf16[384,1280]{1,0:T(8,128)(2,1)S(1)}, u32[]{:S(2)}, u32[]{:S(2)}) collective-permute-start(bf16[384,1280]{1,0:T(8,128)(2,1)S(1)} %pad_maximum_fusion.1), channel_id=1, source_target_pairs={{0,4},{4,0},{8,12},{12,8},{1,5},{5,1},{9,13},{13,9},{2,6},{6,2},{1... | collective-permute-start | bytes 2949128 | tf_op jit(solution)/shard_map/ppermute | solution.py:36
  92.7 11.3 %collective-permute-start = (bf16[384,1536]{1,0:T(8,128)(2,1)S(1)}, bf16[384,1536]{1,0:T(8,128)(2,1)S(1)}, u32[]{:S(2)}, u32[]{:S(2)}) collective-permute-start(bf16[384,1536]{1,0:T(8,128)(2,1)S(1)} %pad_maximum_fusion), channel_id=1, source_target_pairs={{0,4},{4,0},{8,12},{12,8},{1,5},{5,1},{9,13},{13,9},{2,6},{6,2},{1... | collective-permute-start | bytes 3538952 | tf_op jit(solution)/shard_map/ppermute | solution.py:36
  93.0 8.3 %collective-permute-start.8 = (bf16[384,1280]{1,0:T(8,128)(2,1)S(1)}, bf16[384,1280]{1,0:T(8,128)(2,1)S(1)}, u32[]{:S(2)}, u32[]{:S(2)}) collective-permute-start(bf16[384,1280]{1,0:T(8,128)(2,1)S(1)} %pad_maximum_fusion.2), channel_id=1, source_target_pairs={{0,4},{4,0},{8,12},{12,8},{1,5},{5,1},{9,13},{13,9},{2,6},{6,2},{1... | collective-permute-start | bytes 2949128 | tf_op jit(solution)/shard_map/ppermute | solution.py:36
  98.5 4.7 %collective-permute-start.12 = (bf16[384,1280]{1,0:T(8,128)(2,1)S(1)}, bf16[384,1280]{1,0:T(8,128)(2,1)S(1)}, u32[]{:S(2)}, u32[]{:S(2)}) collective-permute-start(bf16[384,1280]{1,0:T(8,128)(2,1)S(1)} %pad_maximum_fusion.3), channel_id=1, source_target_pairs={{0,4},{4,0},{8,12},{12,8},{1,5},{5,1},{9,13},{13,9},{2,6},{6,2},{1... | collective-permute-start | bytes 2949128 | tf_op jit(solution)/shard_map/ppermute | solution.py:36
  98.8 14.1 %collective-permute-start.17 = (bf16[192,1280]{1,0:T(8,128)(2,1)S(1)}, bf16[192,1280]{1,0:T(8,128)(2,1)S(1)}, u32[]{:S(2)}, u32[]{:S(2)}) collective-permute-start(bf16[192,1280]{1,0:T(8,128)(2,1)S(1)} %pad_maximum_fusion.13), channel_id=1, source_target_pairs={{0,8},{4,12},{8,0},{12,4},{1,9},{5,13},{9,1},{13,5},{2,10},{6,14},... | collective-permute-start | bytes 1474568 | tf_op jit(solution)/shard_map/ppermute | solution.py:36
  100.7 22.8 %collective-permute-start.5 = (bf16[192,1280]{1,0:T(8,128)(2,1)S(1)}, bf16[192,1280]{1,0:T(8,128)(2,1)S(1)}, u32[]{:S(2)}, u32[]{:S(2)}) collective-permute-start(bf16[192,1280]{1,0:T(8,128)(2,1)S(1)} %pad_maximum_fusion.7), channel_id=1, source_target_pairs={{0,8},{4,12},{8,0},{12,4},{1,9},{5,13},{9,1},{13,5},{2,10},{6,14},... | collective-permute-start | bytes 1474568 | tf_op jit(solution)/shard_map/ppermute | solution.py:36
  101.6 32.4 %collective-permute-start.9 = (bf16[192,1280]{1,0:T(8,128)(2,1)S(1)}, bf16[192,1280]{1,0:T(8,128)(2,1)S(1)}, u32[]{:S(2)}, u32[]{:S(2)}) collective-permute-start(bf16[192,1280]{1,0:T(8,128)(2,1)S(1)} %pad_maximum_fusion.9), channel_id=1, source_target_pairs={{0,8},{4,12},{8,0},{12,4},{1,9},{5,13},{9,1},{13,5},{2,10},{6,14},... | collective-permute-start | bytes 1474568 | tf_op jit(solution)/shard_map/ppermute | solution.py:36
  103.4 41.1 %collective-permute-start.13 = (bf16[192,1280]{1,0:T(8,128)(2,1)S(1)}, bf16[192,1280]{1,0:T(8,128)(2,1)S(1)}, u32[]{:S(2)}, u32[]{:S(2)}) collective-permute-start(bf16[192,1280]{1,0:T(8,128)(2,1)S(1)} %pad_maximum_fusion.11), channel_id=1, source_target_pairs={{0,8},{4,12},{8,0},{12,4},{1,9},{5,13},{9,1},{13,5},{2,10},{6,14},... | collective-permute-start | bytes 1474568 | tf_op jit(solution)/shard_map/ppermute | solution.py:36
  104.5 63.3 %collective-permute-start.1 = (bf16[192,1536]{1,0:T(8,128)(2,1)S(1)}, bf16[192,1536]{1,0:T(8,128)(2,1)S(1)}, u32[]{:S(2)}, u32[]{:S(2)}) collective-permute-start(bf16[192,1536]{1,0:T(8,128)(2,1)S(1)} %pad_maximum_fusion.5), channel_id=1, source_target_pairs={{0,8},{4,12},{8,0},{12,4},{1,9},{5,13},{9,1},{13,5},{2,10},{6,14},... | collective-permute-start | bytes 1769480 | tf_op jit(solution)/shard_map/ppermute | solution.py:36
  113.1 49.3 %collective-permute-start.18 = (bf16[96,1280]{1,0:T(8,128)(2,1)S(1)}, bf16[96,1280]{1,0:T(8,128)(2,1)S(1)}, u32[]{:S(2)}, u32[]{:S(2)}) collective-permute-start(bf16[96,1280]{1,0:T(8,128)(2,1)S(1)} %fusion.65), channel_id=1, source_target_pairs={{0,8},{4,12},{8,0},{12,4},{1,9},{5,13},{9,1},{13,5},{2,10},{6,14},... | collective-permute-start | bytes 737288 | tf_op jit(solution)/shard_map/ppermute | solution.py:36
  123.6 44.0 %collective-permute-start.6 = (bf16[96,1280]{1,0:T(8,128)(2,1)S(1)}, bf16[96,1280]{1,0:T(8,128)(2,1)S(1)}, u32[]{:S(2)}, u32[]{:S(2)}) collective-permute-start(bf16[96,1280]{1,0:T(8,128)(2,1)S(1)} %fusion.71), channel_id=1, source_target_pairs={{0,8},{4,12},{8,0},{12,4},{1,9},{5,13},{9,1},{13,5},{2,10},{6,14},... | collective-permute-start | bytes 737288 | tf_op jit(solution)/shard_map/ppermute | solution.py:36
  134.2 38.8 %collective-permute-start.10 = (bf16[96,1280]{1,0:T(8,128)(2,1)S(1)}, bf16[96,1280]{1,0:T(8,128)(2,1)S(1)}, u32[]{:S(2)}, u32[]{:S(2)}) collective-permute-start(bf16[96,1280]{1,0:T(8,128)(2,1)S(1)} %fusion.69), channel_id=1, source_target_pairs={{0,8},{4,12},{8,0},{12,4},{1,9},{5,13},{9,1},{13,5},{2,10},{6,14},... | collective-permute-start | bytes 737288 | tf_op jit(solution)/shard_map/ppermute | solution.py:36
  144.7 33.5 %collective-permute-start.14 = (bf16[96,1280]{1,0:T(8,128)(2,1)S(1)}, bf16[96,1280]{1,0:T(8,128)(2,1)S(1)}, u32[]{:S(2)}, u32[]{:S(2)}) collective-permute-start(bf16[96,1280]{1,0:T(8,128)(2,1)S(1)} %fusion.67), channel_id=1, source_target_pairs={{0,8},{4,12},{8,0},{12,4},{1,9},{5,13},{9,1},{13,5},{2,10},{6,14},... | collective-permute-start | bytes 737288 | tf_op jit(solution)/shard_map/ppermute | solution.py:36
  162.5 40.7 %collective-permute-start.19 = (bf16[192,1280]{1,0:T(8,128)(2,1)S(1)}, bf16[192,1280]{1,0:T(8,128)(2,1)S(1)}, u32[]{:S(2)}, u32[]{:S(2)}) collective-permute-start(bf16[192,1280]{1,0:T(8,128)(2,1)S(1)} %pad_maximum_fusion.14), channel_id=1, source_target_pairs={{0,4},{4,0},{8,12},{12,8},{1,5},{5,1},{9,13},{13,9},{2,6},{6,2},{1... | collective-permute-start | bytes 1474568 | tf_op jit(solution)/shard_map/ppermute | solution.py:36
  167.7 16.5 %collective-permute-start.7 = (bf16[192,1280]{1,0:T(8,128)(2,1)S(1)}, bf16[192,1280]{1,0:T(8,128)(2,1)S(1)}, u32[]{:S(2)}, u32[]{:S(2)}) collective-permute-start(bf16[192,1280]{1,0:T(8,128)(2,1)S(1)} %pad_maximum_fusion.8), channel_id=1, source_target_pairs={{0,4},{4,0},{8,12},{12,8},{1,5},{5,1},{9,13},{13,9},{2,6},{6,2},{1... | collective-permute-start | bytes 1474568 | tf_op jit(solution)/shard_map/ppermute | solution.py:36
  168.0 16.1 %collective-permute-start.2 = (bf16[96,1536]{1,0:T(8,128)(2,1)S(1)}, bf16[96,1536]{1,0:T(8,128)(2,1)S(1)}, u32[]{:S(2)}, u32[]{:S(2)}) collective-permute-start(bf16[96,1536]{1,0:T(8,128)(2,1)S(1)} %fusion.63), channel_id=1, source_target_pairs={{0,8},{4,12},{8,0},{12,4},{1,9},{5,13},{9,1},{13,5},{2,10},{6,14},... | collective-permute-start | bytes 884744 | tf_op jit(solution)/shard_map/ppermute | solution.py:36
  173.0 16.0 %collective-permute-start.11 = (bf16[192,1280]{1,0:T(8,128)(2,1)S(1)}, bf16[192,1280]{1,0:T(8,128)(2,1)S(1)}, u32[]{:S(2)}, u32[]{:S(2)}) collective-permute-start(bf16[192,1280]{1,0:T(8,128)(2,1)S(1)} %pad_maximum_fusion.10), channel_id=1, source_target_pairs={{0,4},{4,0},{8,12},{12,8},{1,5},{5,1},{9,13},{13,9},{2,6},{6,2},{1... | collective-permute-start | bytes 1474568 | tf_op jit(solution)/shard_map/ppermute | solution.py:36
  178.3 15.5 %collective-permute-start.15 = (bf16[192,1280]{1,0:T(8,128)(2,1)S(1)}, bf16[192,1280]{1,0:T(8,128)(2,1)S(1)}, u32[]{:S(2)}, u32[]{:S(2)}) collective-permute-start(bf16[192,1280]{1,0:T(8,128)(2,1)S(1)} %pad_maximum_fusion.12), channel_id=1, source_target_pairs={{0,4},{4,0},{8,12},{12,8},{1,5},{5,1},{9,13},{13,9},{2,6},{6,2},{1... | collective-permute-start | bytes 1474568 | tf_op jit(solution)/shard_map/ppermute | solution.py:36
  184.2 14.3 %collective-permute-start.3 = (bf16[192,1536]{1,0:T(8,128)(2,1)S(1)}, bf16[192,1536]{1,0:T(8,128)(2,1)S(1)}, u32[]{:S(2)}, u32[]{:S(2)}) collective-permute-start(bf16[192,1536]{1,0:T(8,128)(2,1)S(1)} %pad_maximum_fusion.6), channel_id=1, source_target_pairs={{0,4},{4,0},{8,12},{12,8},{1,5},{5,1},{9,13},{13,9},{2,6},{6,2},{1... | collective-permute-start | bytes 1769480 | tf_op jit(solution)/shard_map/ppermute | solution.py:36
  209.2 12.2 %collective-permute-start.20 = (bf16[4,24,2048]{2,1,0:T(8,128)(2,1)}, bf16[4,24,2048]{2,1,0:T(8,128)(2,1)}, u32[]{:S(2)}, u32[]{:S(2)}) collective-permute-start(bf16[4,24,2048]{2,1,0:T(8,128)(2,1)} %get-tuple-element.8), channel_id=1, source_target_pairs={{0,1},{1,2},{2,3},{3,0},{4,5},{5,6},{6,7},{7,4},{8,9},{9,10},{10,1... | collective-permute-start | bytes 1179656 | tf_op jit(solution)/shard_map/ppermute | solution.py:66
  210.6 34.6 %collective-permute-start.21 = (bf16[4,24,2048]{2,1,0:T(8,128)(2,1)}, bf16[4,24,2048]{2,1,0:T(8,128)(2,1)}, u32[]{:S(2)}, u32[]{:S(2)}) collective-permute-start(bf16[4,24,2048]{2,1,0:T(8,128)(2,1)} %get-tuple-element.10), channel_id=1, source_target_pairs={{0,2},{1,3},{2,0},{3,1},{4,6},{5,7},{6,4},{7,5},{8,10},{9,11},{10,... | collective-permute-start | bytes 1179656 | tf_op jit(solution)/shard_map/ppermute | solution.py:66
  213.2 34.4 %collective-permute-start.22 = (bf16[4,24,2048]{2,1,0:T(8,128)(2,1)S(1)}, bf16[4,24,2048]{2,1,0:T(8,128)(2,1)}, u32[]{:S(2)}, u32[]{:S(2)}) collective-permute-start(bf16[4,24,2048]{2,1,0:T(8,128)(2,1)S(1)} %get-tuple-element.9), channel_id=1, source_target_pairs={{0,3},{1,0},{2,1},{3,2},{4,7},{5,4},{6,5},{7,6},{8,11},{9,8},{10,9... | collective-permute-start | bytes 1179656 | tf_op jit(solution)/shard_map/ppermute | solution.py:66
Sparse Core Ops, SparseCore 0:
  11.0 37.2 all-gather.1

commit v2 on v1

--- a/solution.py
+++ b/solution.py
@@ -1,7 +1,11 @@
+import functools
+
 import jax
 import jax.numpy as jnp
 import numpy as np
 from jax import lax
+from jax.experimental import pallas as pl
+from jax.experimental.pallas import tpu as pltpu
 from jax.sharding import PartitionSpec as P
 
 BLOCK = 128
@@ -15,6 +19,227 @@
     sizes = [(tiles // parts + (1 if i < tiles % parts else 0)) * step for i in range(parts)]
     sizes[-1] += units - sum(sizes)
     return sizes
+
+
+PASSES = 2
+WIDTH = 512
+LAG_ACT, LAG_FWD, LAG_DOWN = 3, 6, 7
+WSLOTS = 3
+KSLOTS = 4
+
+
+def fused_kernel(z, n_iter, per_pass, tokens, keep, wg, wu, wd, out,
+                 rows_buf, wg_buf, wu_buf, wd_buf, held, core_out, core_in, x_out, x_in, hid, acc, z_out, z_in,
+                 wg_sem, wu_sem, wd_sem, ag_s, ag_r, core_s, core_r, x_s, x_r, hx_s, hx_r, hc_s, hc_r, z_s, z_r):
+    f32, bf16 = jnp.float32, jnp.bfloat16
+    me = lax.axis_index("mp")
+    mz = lax.axis_index("hidden")
+    k, xb = me % 2, me // 2
+    core_peer = xb * 2 + (1 - k)
+    x_peer = (1 - xb) * 2 + k
+    b = rows_buf.shape[2]
+    w = WIDTH
+    mesh_id = pl.DeviceIdType.MESH
+
+    def place(j):
+        return ((j // 2 + 1 - k) % 2) * 2 + (j + 1 - xb) % 2
+
+    def wg_copy(i):
+        c = i % per_pass
+        return pltpu.make_async_copy(wg.at[:, pl.ds(pl.multiple_of(c * w, w), w)], wg_buf.at[i % WSLOTS], wg_sem.at[i % WSLOTS])
+
+    def wu_copy(i):
+        c = i % per_pass
+        return pltpu.make_async_copy(wu.at[:, pl.ds(pl.multiple_of(c * w, w), w)], wu_buf.at[i % WSLOTS], wu_sem.at[i % WSLOTS])
+
+    def wd_copy(i):
+        c = i % per_pass
+        return pltpu.make_async_copy(wd.at[pl.ds(pl.multiple_of(c * w, w), w), :], wd_buf.at[i % WSLOTS], wd_sem.at[i % WSLOTS])
+
+    def remote(src, dst, s, r, device):
+        return pltpu.make_async_remote_copy(src_ref=src, dst_ref=dst, send_sem=s, recv_sem=r, device_id=device, device_id_type=mesh_id)
+
+    def ag_copy(q, s):
+        here = rows_buf.at[q, place(mz)]
+        return remote(here, here, ag_s.at[q, s - 1], ag_r.at[q, s - 1], {"hidden": (mz + s) % z})
+
+    def core_copy(i):
+        return remote(core_out.at[i], core_in.at[i], core_s.at[i], core_r.at[i], {"mp": core_peer})
+
+    def x_copy(i):
+        return remote(x_out.at[i], x_in.at[i], x_s.at[i], x_r.at[i], {"mp": x_peer})
+
+    def hx_copy(i):
+        return remote(hid.at[i, pl.ds(3 * b, b)], hid.at[i, pl.ds(2 * b, b)], hx_s.at[i], hx_r.at[i], {"mp": x_peer})
+
+    def hc_copy(i):
+        return remote(hid.at[i, pl.ds(2 * b, 2 * b)], hid.at[i, pl.ds(0, 2 * b)], hc_s.at[i], hc_r.at[i], {"mp": core_peer})
+
+    def z_copy(q, s):
+        return remote(z_out.at[q, s - 1], z_in.at[q, s - 1], z_s.at[q, s - 1], z_r.at[q, s - 1], {"hidden": (mz + s) % z})
+
+    for i in range(min(WSLOTS, n_iter)):
+        wg_copy(i).start()
+        wu_copy(i).start()
+    for i in range(min(WSLOTS, n_iter)):
+        wd_copy(i).start()
+
+    barrier = pltpu.get_barrier_semaphore()
+    pl.semaphore_signal(barrier, inc=1, device_id={"mp": core_peer}, device_id_type=mesh_id)
+    pl.semaphore_signal(barrier, inc=1, device_id={"mp": x_peer}, device_id_type=mesh_id)
+    for s in range(1, z):
+        pl.semaphore_signal(barrier, inc=1, device_id={"hidden": (mz + s) % z}, device_id_type=mesh_id)
+
+    mine = place(mz)
+    for q in range(PASSES):
+        for j in range(keep.shape[1]):
+            piece = tokens[q * b:(q + 1) * b, j * BLOCK:(j + 1) * BLOCK].astype(f32)
+            factor = keep[q * b:(q + 1) * b, j:j + 1].astype(f32)
+            rows_buf[q, mine, :, j * BLOCK:(j + 1) * BLOCK] = (piece * factor).astype(bf16)
+
+    pl.semaphore_wait(barrier, 2 + z - 1)
+    for q in range(PASSES):
+        for s in range(1, z):
+            ag_copy(q, s).start()
+
+    def project(i):
+        q = i // per_pass
+
+        @pl.when(i % per_pass == 0)
+        def _():
+            for s in range(1, z):
+                ag_copy(q, s).wait_recv()
+
+        rows = rows_buf[q].reshape(4 * b, rows_buf.shape[3])
+        wg_copy(i).wait()
+        slot = i % WSLOTS
+        gate = jnp.dot(rows, wg_buf[slot], preferred_element_type=f32)
+        core_out[i, :, 0:w] = gate[:2 * b].astype(bf16)
+        held[i % KSLOTS, :, 0:w] = gate[2 * b:]
+        wu_copy(i).wait()
+        up = jnp.dot(rows, wu_buf[slot], preferred_element_type=f32)
+        core_out[i, :, w:2 * w] = up[:2 * b].astype(bf16)
+        core_copy(i).start()
+        held[i % KSLOTS, :, w:2 * w] = up[2 * b:]
+
+        @pl.when(i + WSLOTS < n_iter)
+        def _():
+            wg_copy(i + WSLOTS).start()
+            wu_copy(i + WSLOTS).start()
+
+    def combine(i):
+        core_copy(i).wait_recv()
+        slot = i % KSLOTS
+        x_out[i] = (held[slot, 0:b] + core_in[i, 0:b].astype(f32)).astype(bf16)
+        x_copy(i).start()
+        held[slot, b:2 * b] = held[slot, b:2 * b] + core_in[i, b:2 * b].astype(f32)
+
+    def act(i):
+        x_copy(i).wait_recv()
+        slot = i % KSLOTS
+        gate = held[slot, b:2 * b, 0:w] + x_in[i, :, 0:w].astype(f32)
+        up = held[slot, b:2 * b, w:2 * w] + x_in[i, :, w:2 * w].astype(f32)
+        hid[i, 3 * b:4 * b] = (gate / (1.0 + jnp.exp(-gate)) * up).astype(bf16)
+        hx_copy(i).start()
+
+    def forward(i):
+        hx_copy(i).wait_recv()
+        hc_copy(i).start()
+
+    def down(i):
+        q = i // per_pass
+        hc_copy(i).wait_recv()
+        wd_copy(i).wait()
+        part = jnp.dot(hid[i], wd_buf[i % WSLOTS], preferred_element_type=f32).reshape(4, b, acc.shape[3])
+
+        @pl.when(i % per_pass == 0)
+        def _():
+            acc[q] = part
+
+        @pl.when(i % per_pass != 0)
+        def _():
+            acc[q] = acc[q] + part
+
+        @pl.when(i + WSLOTS < n_iter)
+        def _():
+            wd_copy(i + WSLOTS).start()
+
+        @pl.when(i % per_pass == per_pass - 1)
+        def _():
+            for s in range(1, z):
+                z_out[q, s - 1] = acc[q, place((mz + s) % z)].astype(bf16)
+                z_copy(q, s).start()
+
+    def step(t, carry):
+        for stage, lag in ((project, 0), (combine, 1), (act, LAG_ACT), (forward, LAG_FWD), (down, LAG_DOWN)):
+            @pl.when(jnp.logical_and(t >= lag, t < n_iter + lag))
+            def _(stage=stage, lag=lag):
+                stage(t - lag)
+        return carry
+
+    lax.fori_loop(0, n_iter + LAG_DOWN, step, 0)
+
+    def drain(i, carry):
+        core_copy(i).wait_send()
+        x_copy(i).wait_send()
+        hx_copy(i).wait_send()
+        hc_copy(i).wait_send()
+        return carry
+
+    lax.fori_loop(0, n_iter, drain, 0)
+    for q in range(PASSES):
+        total = acc[q, mine]
+        for s in range(1, z):
+            ag_copy(q, s).wait_send()
+            z_copy(q, s).wait()
+            total = total + z_in[q, s - 1].astype(f32)
+        out[q * b:(q + 1) * b, :] = total.astype(bf16)
+
+
+def fused(tokens, block_mask, gate_weight, up_weight, down_weight):
+    z = lax.axis_size("hidden")
+    rows, features = tokens.shape
+    units = gate_weight.shape[1]
+    cols = down_weight.shape[1]
+    b = rows // PASSES
+    per_pass = units // WIDTH
+    n = per_pass * PASSES
+    f32, bf16 = jnp.float32, jnp.bfloat16
+    dma = pltpu.SemaphoreType.DMA
+    flops = 2 * rows * z * units * (2 * features + cols)
+    vmem = pl.BlockSpec(memory_space=pltpu.VMEM)
+    hbm = pl.BlockSpec(memory_space=pl.ANY)
+    return pl.pallas_call(
+        functools.partial(fused_kernel, z, n, per_pass),
+        out_shape=jax.ShapeDtypeStruct((rows, cols), bf16),
+        in_specs=[vmem, vmem, hbm, hbm, hbm],
+        out_specs=vmem,
+        scratch_shapes=[
+            pltpu.VMEM((PASSES, z, b, features), bf16),
+            pltpu.VMEM((WSLOTS, features, WIDTH), bf16),
+            pltpu.VMEM((WSLOTS, features, WIDTH), bf16),
+            pltpu.VMEM((WSLOTS, WIDTH, cols), bf16),
+            pltpu.VMEM((KSLOTS, 2 * b, 2 * WIDTH), f32),
+            pltpu.VMEM((n, 2 * b, 2 * WIDTH), bf16),
+            pltpu.VMEM((n, 2 * b, 2 * WIDTH), bf16),
+            pltpu.VMEM((n, b, 2 * WIDTH), bf16),
+            pltpu.VMEM((n, b, 2 * WIDTH), bf16),
+            pltpu.VMEM((n, 4 * b, WIDTH), bf16),
+            pltpu.VMEM((PASSES, z, b, cols), f32),
+            pltpu.VMEM((PASSES, z - 1, b, cols), bf16),
+            pltpu.VMEM((PASSES, z - 1, b, cols), bf16),
+            dma((WSLOTS,)), dma((WSLOTS,)), dma((WSLOTS,)),
+            dma((PASSES, z - 1)), dma((PASSES, z - 1)),
+            dma((n,)), dma((n,)), dma((n,)), dma((n,)), dma((n,)), dma((n,)), dma((n,)), dma((n,)),
+            dma((PASSES, z - 1)), dma((PASSES, z - 1)),
+        ],
+        compiler_params=pltpu.CompilerParams(
+            collective_id=0, has_side_effects=True, vmem_limit_bytes=60 * 1024 * 1024
+        ),
+        cost_estimate=pl.CostEstimate(
+            flops=flops, bytes_accessed=2 * PASSES * units * (2 * features + cols), transcendentals=rows * z * units
+        ),
+    )(tokens, block_mask, gate_weight, up_weight, down_weight)
 
 
 def local(tokens, block_mask, gate_weight, up_weight, down_weight):
@@ -25,6 +250,8 @@
     rows, features = tokens.shape
     cols = down_weight.shape[1]
     units = gate_weight.shape[1]
+    if n == 4 and z == 4 and units % WIDTH == 0 and rows % (16 * PASSES) == 0:
+        return fused(tokens, block_mask, gate_weight, up_weight, down_weight)
     r = rows // n
     bits = [1 << i for i in range(n.bit_length() - 1)]
     masks = np.array(

time: 258 us -> 145 us (0.56)
  Pallas kernels: 0 us -> 140 us
  waiting for transfers between devices: 140 us -> 0 us
  matrix products: 71.6 us -> 0 us
  starting transfers between devices: 19.2 us -> 0 us
  between operations: 14 us -> 0.01 us
  other arithmetic: 8.34 us -> 0 us
    pallas_call x0 -> x1, Pallas kernels: none -> 140 us  [fused(): pl.pallas_call(functools.partial(fused_kernel, z, n, per_pass), out_shape...]
    ppermute x23 -> x0, waiting for transfers between devices: 103 us -> none  [the longest x20 69 us: swap(): return lax.ppermute(x, 'mp', [(i, i ^ bit) for i in range(n)])]
    dot_general x15 -> x0, matrix products: 71.6 us -> none  [the longest x5 24.2 us: local(): jnp.dot(all_rows, up_weight[:, start:stop], preferred_element_type=jnp.fl...]
    all_gather x1 -> x0, waiting for transfers between devices: 36.7 us -> none  [local(): lax.all_gather(masked, 'hidden', axis=1, tiled=True)]
    ppermute x23 -> x0, starting transfers between devices: 19.2 us -> none  [the longest x20 15.3 us: swap(): return lax.ppermute(x, 'mp', [(i, i ^ bit) for i in range(n)])]
    unnamed x4 -> x2, local copies, waits for them, and re-layouts: 0.01 us -> 3.17 us
    convert_element_type x7 -> x0, other arithmetic: 3.11 us -> none  [the longest x1 1.45 us: local(): total.astype(jnp.bfloat16)]
  transfers between devices with their start and end apart: 24 -> 0, of which waited for: 13 -> 0; matrix products, arithmetic and copies ran while one was open for 11% -> 0% of each run, Pallas kernels for 0% -> 0%
where the time goes in v2:
time: 145 us; the launch traced here: 143 us
  Pallas kernels  140 us (97%)
  local copies, waits for them, and re-layouts  3.17 us (2%)
    pallas_call x1, Pallas kernels, fused(): pl.pallas_call(functools.partial(fused_kernel, z, n, per_pass), out_shape...  140 us
    unnamed x2, local copies, waits for them, and re-layouts  3.17 us

profile of v2, /device:TPU:8, one launch (start us, length us, event | category | flops | bytes accessed | tf_op | source)
XLA Modules:
  0.0 143.4 jit_solution(9760439152576862768)
XLA Ops:
  0.0 1.4 copy.6.keep
  1.4 140.2 %shard_map.55 = bf16[96,2048]{1,0:T(8,128)(2,1)} custom-call(bf16[96,2048]{1,0:T(8,128)(2,1)} %tokens.1, s32[96,16]{1,0:T(8,128)} %copy.6.keep, bf16[2048,6656]{1,0:T(8,128)(2,1)} %wg.1, bf16[2048,6656]{1,0:T(8,128)(2,1)} %wu.1, bf16[6656,2048]{1,0:T(8,128)(2,1)} %wd.1), custom_call_target="tpu_custom_call" | custom-call | flops 31406948352 | bytes 163577856 | tf_op jit(solution)/shard_map/pallas_call | solution.py:212
  141.7 1.8 %copy.8 = bf16[96,2048]{1,0:T(8,128)(2,1)} copy(bf16[96,2048]{1,0:T(8,128)(2,1)} %shard_map.55) | data formatting | bytes 786432

commit v3 on v2

--- a/solution.py
+++ b/solution.py
@@ -21,7 +21,7 @@
     return sizes
 
 
-PASSES = 2
+PASSES = 3
 WIDTH = 512
 LAG_ACT, LAG_FWD, LAG_DOWN = 3, 6, 7
 WSLOTS = 3
@@ -98,9 +98,8 @@
             rows_buf[q, mine, :, j * BLOCK:(j + 1) * BLOCK] = (piece * factor).astype(bf16)
 
     pl.semaphore_wait(barrier, 2 + z - 1)
-    for q in range(PASSES):
-        for s in range(1, z):
-            ag_copy(q, s).start()
+    for s in range(1, z):
+        ag_copy(0, s).start()
 
     def project(i):
         q = i // per_pass
@@ -109,6 +108,11 @@
         def _():
             for s in range(1, z):
                 ag_copy(q, s).wait_recv()
+
+            @pl.when(q + 1 < PASSES)
+            def _():
+                for s in range(1, z):
+                    ag_copy(q + 1, s).start()
 
         rows = rows_buf[q].reshape(4 * b, rows_buf.shape[3])
         wg_copy(i).wait()

time: 145 us -> 126 us (0.87)
  Pallas kernels: 140 us -> 122 us
    pallas_call x1, Pallas kernels: 140 us -> 122 us  [fused(): pl.pallas_call(functools.partial(fused_kernel, z, n, per_pass), out_shape...]
where the time goes in v3:
time: 126 us; the launch traced here: 125 us
  Pallas kernels  122 us (97%)
  local copies, waits for them, and re-layouts  3.17 us (3%)
    pallas_call x1, Pallas kernels, fused(): pl.pallas_call(functools.partial(fused_kernel, z, n, per_pass), out_shape...  122 us
    unnamed x2, local copies, waits for them, and re-layouts  3.17 us

profile of v3, /device:TPU:8, one launch (start us, length us, event | category | flops | bytes accessed | tf_op | source)
XLA Modules:
  0.0 124.9 jit_solution(16942779529201311365)
XLA Ops:
  0.0 1.4 %copy.6.keep = s32[96,16]{1,0:T(8,128)} copy(s32[96,16]{0,1:T(8,128)} %param.6) | data formatting | bytes 12288 | tf_op args[1]
  1.4 121.7 %shard_map.55 = bf16[96,2048]{1,0:T(8,128)(2,1)} custom-call(bf16[96,2048]{1,0:T(8,128)(2,1)} %tokens.1, s32[96,16]{1,0:T(8,128)} %copy.6.keep, bf16[2048,6656]{1,0:T(8,128)(2,1)} %wg.1, bf16[2048,6656]{1,0:T(8,128)(2,1)} %wu.1, bf16[6656,2048]{1,0:T(8,128)(2,1)} %wd.1), custom_call_target="tpu_custom_call" | custom-call | flops 31406948352 | bytes 245366784 | tf_op jit(solution)/shard_map/pallas_call | solution.py:216
  123.1 1.8 %copy.8 = bf16[96,2048]{1,0:T(8,128)(2,1)} copy(bf16[96,2048]{1,0:T(8,128)(2,1)} %shard_map.55) | data formatting | bytes 786432
